TPU v7x, 32 devices: a whole 2x2x4 slice. The times are simulated.
32 devices in a mesh: rows: 8 (over z, y), dp: 4 (over x, core).
Axes of the slice: x: 2, y: 2, z: 4, core: 2. Of those that a mesh axis runs over, the one named last changes fastest.
Arguments:
- tokens: bfloat16 [16384, 512], P(('rows', 'dp')), may hold values from -6 to 6
- out_grad: bfloat16 [16384, 512], P(('rows', 'dp')), may hold values from -6 to 6
- seq_lengths: int32 [32, 4], P(('rows', 'dp')), may hold values from 1 to 256, 512 in all within a row
- owners: int32 [16384, 1], P(('rows', 'dp')), may hold values from 0 to 7; in each aligned block of 512 rows (0 to 511, 512 to 1023, ...) at most 256 rows name the same one
- slots: int32 [16384], P(('rows', 'dp')), may hold values from 0 to 127
- w_in: bfloat16 [512, 1024], replicated, may hold values from -0.25 to 0.25
- w_out: bfloat16 [512, 256], replicated, may hold values from -0.375 to 0.375
- emb_rows: float32 [1024, 512], P('rows'), may hold values from -0.6 to 0.6
- emb_mom: float32 [1024, 512], P('rows'), may hold values from -0.6 to 0.6
- emb_var: float32 [1024], P('rows'), may hold values from 0.01 to 0.1
Outputs:
- new_rows: float32 [1024, 512], P('rows')
- new_mom: float32 [1024, 512], P('rows')
- new_var: float32 [1024], P('rows')
- w_in_grad: float32 [512, 1024], P('rows')
- w_out_grad: float32 [512, 256], P('rows')
Inputs may be any that keep to these rules, and one draw needn't show every extreme that they name: `seq_lengths`: each row sums to 512; its largest entry is exactly 256. `owners`: among the 512 tokens of one device at most 256 name the same owner; some device reaches 256.
All inputs are finite; a program needn't handle non-finite values.
Results may differ from a plain program's by a relative error of at most 0.015.
Values may be sent and summed in bfloat16 or wider, within the bound.
A program may use at most 64 MiB of HBM per device.

v0:
```python
import jax
import jax.numpy as jnp
from jax import lax
from jax.sharding import PartitionSpec as P

HEADS = 4
HEAD_DIM = 64
HW = 256
MAXLEN = 256


norm_eps = 1e-06
beta_one = 0.9
beta_two = 0.99
learn_rate = 0.05
adam_eps = 1e-08
bias_one = 1.0 - 0.9**10
bias_two = 1.0 - 0.99**10


def layer_norm(values):
    average = jnp.mean(values, axis=-1, keepdims=True)
    centered = values - average
    spread = jnp.mean(centered * centered, axis=-1, keepdims=True)
    return centered * lax.rsqrt(spread + norm_eps)


def allowed_mask(lengths, tok_count):
    ends = jnp.cumsum(lengths)
    position = jnp.arange(tok_count, dtype=jnp.int32)
    segment = jnp.sum((position[:, None] >= ends[None, :]).astype(jnp.int32), axis=1)
    same = segment[:, None] == segment[None, :]
    causal = position[None, :] <= position[:, None]
    return (same & causal).astype(jnp.float32)


def core(pre, allowed):
    tok_count = pre.shape[0]
    proj = jax.nn.silu(pre).astype(jnp.bfloat16)
    upart, vpart, qpart, kpart = jnp.split(proj, 4, axis=1)
    queries = qpart.reshape(tok_count, HEADS, HEAD_DIM)
    keys_part = kpart.reshape(tok_count, HEADS, HEAD_DIM)
    values_part = vpart.reshape(tok_count, HEADS, HEAD_DIM)
    scores = jnp.einsum(
        "thd,shd->hts", queries, keys_part, preferred_element_type=jnp.float32
    ) * HEAD_DIM ** (-0.5)
    weights = (jax.nn.silu(scores) * allowed[None] / MAXLEN).astype(jnp.bfloat16)
    attn = jnp.einsum(
        "hts,shd->thd", weights, values_part, preferred_element_type=jnp.float32
    ).reshape(tok_count, HW)
    return (layer_norm(attn) * upart.astype(jnp.float32)).astype(jnp.bfloat16)


def row_adam(rows_now, mom_now, var_now, grad, counts):
    touched = counts > 0.5
    mom_next = beta_one * mom_now + (1.0 - beta_one) * grad
    var_next = beta_two * var_now + (1.0 - beta_two) * jnp.mean(grad * grad, axis=1)
    advance = mom_next / bias_one / (jnp.sqrt(var_next / bias_two)[:, None] + adam_eps)
    rows_next = rows_now - learn_rate * advance
    return (
        jnp.where(touched[:, None], rows_next, rows_now),
        jnp.where(touched[:, None], mom_next, mom_now),
        jnp.where(touched, var_next, var_now),
    )


def local(tokens, out_grad, seq_lengths, owners, slots, w_in, w_out, emb_rows, emb_mom, emb_var):
    tok_count = tokens.shape[0]
    width = tokens.shape[1]
    allowed = allowed_mask(seq_lengths[0], tok_count)
    normed_exact, norm_back = jax.vjp(layer_norm, tokens.astype(jnp.float32))
    normed = normed_exact.astype(jnp.bfloat16)
    pre = jnp.dot(normed, w_in, preferred_element_type=jnp.float32)
    y_out, core_back = jax.vjp(lambda inner: core(inner, allowed), pre)
    y_grad = jnp.dot(out_grad, w_out, preferred_element_type=jnp.float32).astype(jnp.bfloat16)
    pre_grad_b = core_back(y_grad)[0].astype(jnp.bfloat16)
    normed_grad = lax.dot_general(
        pre_grad_b, w_in, (((1,), (1,)), ((), ())), preferred_element_type=jnp.float32
    )
    emb_grad = (norm_back(normed_grad)[0] + out_grad.astype(jnp.float32)).astype(jnp.bfloat16)
    contract = (((0,), (0,)), ((), ()))
    in_cols = w_in.shape[1]
    owner_count = lax.axis_size("rows")
    weight_share = lax.psum_scatter(
        jnp.concatenate(
            [
                lax.dot_general(normed, pre_grad_b, contract, preferred_element_type=jnp.float32),
                lax.dot_general(out_grad, y_out, contract, preferred_element_type=jnp.float32),
            ],
            axis=1,
        ),
        "rows",
        scatter_dimension=0,
        tiled=True,
    )
    weight_share = lax.psum(weight_share, "dp")
    w_in_grad = weight_share[:, :in_cols]
    w_out_grad = weight_share[:, in_cols:]
    capacity = max(2, 4 * tok_count // owner_count)
    buffer_rows = owner_count * capacity
    owner_of = owners[:, 0]
    position = jnp.arange(tok_count, dtype=jnp.int32)
    earlier = jnp.sum(
        ((owner_of[:, None] == owner_of[None, :]) & (position[None, :] < position[:, None])).astype(
            jnp.int32
        ),
        axis=1,
    )
    position_to = owner_of * capacity + earlier
    chosen = position_to[None, :] == jnp.arange(buffer_rows, dtype=jnp.int32)[:, None]
    outgoing = jnp.dot(
        chosen.astype(jnp.bfloat16), emb_grad, preferred_element_type=jnp.float32
    ).astype(jnp.bfloat16)
    outgoing = outgoing.reshape(owner_count, capacity, width)
    out_slots = (jnp.sum(jnp.where(chosen, slots[None, :] + 1, 0), axis=1) - 1).reshape(
        owner_count, capacity
    )
    arrived, arrived_slots = (
        lax.all_to_all(outgoing, "rows", split_axis=0, concat_axis=0, tiled=True),
        lax.all_to_all(out_slots, "rows", split_axis=0, concat_axis=0, tiled=True),
    )
    received = arrived.reshape(buffer_rows, width)
    got_slots = arrived_slots.reshape(buffer_rows)
    slot_count = emb_rows.shape[0]
    matches = got_slots[None, :] == jnp.arange(slot_count, dtype=jnp.int32)[:, None]
    grad_part = jnp.dot(matches.astype(jnp.bfloat16), received, preferred_element_type=jnp.float32)
    count_part = jnp.sum(matches.astype(jnp.float32), axis=1)
    grad_all, count_all = lax.psum((grad_part, count_part), "dp")
    new_rows, new_mom, new_var = row_adam(emb_rows, emb_mom, emb_var, grad_all, count_all)
    return (new_rows, new_mom, new_var, w_in_grad, w_out_grad)


def solution(mesh):
    in_specs = (
        P(("rows", "dp"), None),
        P(("rows", "dp"), None),
        P(("rows", "dp"), None),
        P(("rows", "dp"), None),
        P(("rows", "dp")),
        P(),
        P(),
        P("rows", None),
        P("rows", None),
        P("rows"),
    )
    out_specs = (P("rows", None), P("rows", None), P("rows"), P("rows", None), P("rows", None))
    return jax.shard_map(local, mesh=mesh, in_specs=in_specs, out_specs=out_specs, check_vma=False)
```

profile of v0, /device:TPU:0, one launch (start us, length us, event | category | flops | bytes accessed | tf_op | source)
XLA Modules:
  0.0 187.7 jit_solution(2320132211699484735)
XLA Ops:
  8.3 1.2 fusion.21
  9.5 1.2 fusion.20
  11.2 2.3 %multiply_convert_fusion.1 = (bf16[512,1024]{1,0:T(8,128)(2,1)S(1)}, f32[512,1024]{1,0:T(8,128)}) fusion(bf16[512,1024]{1,0:T(8,128)(2,1)S(1)} %copy-done, bf16[512,512]{0,1:T(8,128)(2,1)S(1)} %copy.42, f32[512]{0:T(512)S(1)} %fusion.37, f32[512]{0:T(512)S(1)} %broadcast_multiply_fusion.1), kind=kOutput, calls=%fused_computation.17 | convolution fusion | flops 540540928 | bytes 4722688 | tf_op jit(solution)/shard_map/dot_general | solution.py:73
  15.1 4.8 %multiply_convert_fusion = (bf16[4,512,512]{2,1,0:T(8,128)(2,1)S(1)}, f32[4,512,512]{2,1,0:T(8,128)}) fusion(f32[512,512]{1,0:T(8,128)} %fusion.21, bf16[512,4,64]{0,2,1:T(8,128)(2,1)S(1)} %bitcast.55, bf16[512,4,64]{0,2,1:T(8,128)(2,1)S(1)} %bitcast.57), kind=kOutput, calls=%fused_computation.4 | convolution fusion | flops 142606336 | bytes 7864320 | tf_op jit(solution)/shard_map/jvp(thd,shd->hts)/dot_general | solution.py:44
  19.9 1.3 copy-done.1
  22.3 1.4 multiply_reduce_fusion
  23.7 1.9 %fusion.40 = (f32[512]{0:T(512)S(1)}, f32[512,256]{1,0:T(8,128)S(1)}, bf16[512,256]{1,0:T(8,128)(2,1)}) fusion(f32[512]{0:T(512)S(1)} %get-tuple-element.16, f32[512,256]{1,0:T(8,128)S(1)} %copy.46, f32[512]{0:T(512)S(1)} %broadcast_multiply_fusion, f32[512]{0:T(512)S(1)} %get-tuple-element.15, f32[512,256]{1,0:T(8,128)S(1)} %get-tuple-element.26, ...), kind=kLoop, calls=%fused_computation.88 | loop fusion | flops 1441280 | bytes 2105344 | tf_op jit(solution)/shard_map/transpose(jvp())/reduce_sum | solution.py:23
  27.6 2.9 %fusion.45 = bf16[4,64,512]{2,1,0:T(8,128)(2,1)} fusion(bf16[4,64,512]{2,1,0:T(8,128)(2,1)S(1)} %bitcast.64, bf16[4,512,512]{2,1,0:T(8,128)(2,1)} %copy-done.1), kind=kOutput, calls=%fused_computation.93 | convolution fusion | flops 134217728 | bytes 2621440 | tf_op jit(solution)/shard_map/transpose(jvp(hts,shd->thd))/dot_general | solution.py:48
  30.5 4.2 %fusion.2 = bf16[4,512,512]{2,1,0:T(8,128)(2,1)S(1)} fusion(f32[4,512,512]{2,1,0:T(8,128)} %get-tuple-element.22, f32[512,512]{1,0:T(8,128)S(1)} %copy-done.12, bf16[4,64,512]{2,1,0:T(8,128)(2,1)} %bitcast.65, bf16[512,4,64]{0,2,1:T(8,128)(2,1)S(1)} %bitcast.60), kind=kOutput, calls=%fused_computation.3 | convolution fusion | flops 148897792 | bytes 7864320 | tf_op jit(solution)/shard_map/transpose(jvp(hts,shd->thd))/dot_general | solution.py:48
  35.5 1.2 fusion.43
  36.7 2.3 %convolution_bitcast_fusion = f32[512,256]{1,0:T(8,128)} fusion(bf16[512,512]{1,0:T(8,128)(2,1)S(1)} %copy-done.2, f32[512,256]{1,0:T(8,128)S(1)} %copy.46, f32[512]{0:T(512)S(1)} %get-tuple-element.15, f32[512]{0:T(512)S(1)} %broadcast_multiply_fusion, bf16[512,1024]{1,0:T(8,128)(2,1)} %copy-done.3), kind=kOutput, calls=%fused_computation.27 | convolution fusion | flops 134873088 | bytes 1839104 | tf_op jit(solution)/shard_map/dot_general | solution.py:88
  41.6 2.7 %fusion.6 = bf16[512,1024]{1,0:T(8,128)(2,1)S(1)} fusion(f32[512,1024]{1,0:T(8,128)} %get-tuple-element.20, bf16[512,256]{1,0:T(8,128)(2,1)} %copy.51, bf16[512,256]{1,0:T(8,128)(2,1)} %copy.50, bf16[512,256]{1,0:T(8,128)(2,1)} %copy.49, bf16[512,256]{1,0:T(8,128)(2,1)} %get-tuple-element.9), kind=kLoop, calls=%fused_computation.15 | loop fusion | flops 9437184 | bytes 4194304 | tf_op jit(solution)/shard_map/convert_element_type | solution.py:76
  45.3 1.7 pad_maximum_fusion
  49.0 7.3 %all-to-all-start = ((s32[8,1,256]{2,1,0:T(1,128)}), s32[8,1,256]{2,1,0:T(1,128)S(1)}, u32[]{:S(2)}, u32[]{:S(2)}) async-start(s32[8,1,256]{2,1,0:T(1,128)} %bitcast.1), calls=%async_computation | async-start | bytes 16384 | tf_op jit(solution)/shard_map/all_to_all | solution.py:120
  58.6 2.7 %fusion.4 = bf16[2048,512]{1,0:T(8,128)(2,1)} fusion(s32[512]{0:T(512)S(1)} %get-tuple-element.29, bf16[512,512]{0,1:T(8,128)(2,1)S(1)} %copy-done.14, f32[512]{0:T(512)S(1)} %negate_multiply_fusion, bf16[512,512]{0,1:T(8,128)(2,1)S(1)} %copy.42, f32[512,512]{0,1:T(8,128)S(1)} %get-tuple-element.28, f32[512]{0:T(512)S(1)} %multiply_multiply_fusion, ...), kind=kOutput, calls=%fused_computation.10 | convolution fusion | flops 1078460416 | bytes 4204544 | tf_op jit(solution)/shard_map/dot_general | solution.py:111
  61.4 1.5 all-to-all-done
  62.8 70.2 %all_to_all.11 = bf16[8,256,512]{2,1,0:T(8,128)(2,1)S(1)} all-to-all(bf16[8,256,512]{2,1,0:T(8,128)(2,1)} %bitcast.54), channel_id=1, replica_groups=mesh['rows'=8,'dp'=4] {'rows'}, dimensions={0} | all-to-all | bytes 4194304 | tf_op jit(solution)/shard_map/all_to_all | solution.py:119
  133.1 1.2 fusion.17
  134.2 4.0 %reduce-scatter.2.cloned.1.call-done = f32[64,1280]{1,0:T(8,128)} async-done(((f32[512,1280]{1,0:T(8,128)}), f32[64,1280]{1,0:T(8,128)}) %reduce-scatter.2.cloned.1.call-update) | async-done | bytes 327696 | tf_op jit(solution)/shard_map/reduce_scatter | solution.py:84
  138.5 6.8 %psum.21 = f32[128]{0:T(128)S(1)} all-reduce(f32[128]{0:T(128)S(1)} %convert_reduce_fusion.1), channel_id=1, replica_groups=mesh['rows'=8,'dp'=4] {'dp'}, use_global_device_ids=true, to_apply=%region_3.4 | all-reduce | flops 128 | bytes 1024 | tf_op jit(solution)/shard_map/psum | solution.py:128
  145.3 28.9 %all-reduce.3.cloned.1.call-done = (f32[128,512]{1,0:T(8,128)}, f32[64,1280]{1,0:T(8,128)}) async-done(((f32[128,512]{1,0:T(8,128)}, f32[64,1280]{1,0:T(8,128)}), (f32[128,512]{1,0:T(8,128)}, f32[64,1280]{1,0:T(8,128)})) %all-reduce.3.cloned.1.call-update) | async-done | bytes 589840 | tf_op jit(solution)/shard_map/psum | solution.py:128
  174.3 1.7 slice.8
  175.9 1.5 slice.9
  179.0 1.9 fusion.35
  (80 shorter events, 16.6 us)
Async XLA Ops:
  7.2 4.0 %copy-start = (bf16[512,1024]{1,0:T(8,128)(2,1)S(1)}, bf16[512,1024]{1,0:T(8,128)(2,1)}, u32[]{:S(2)}) copy-start(bf16[512,1024]{1,0:T(8,128)(2,1)} %param.15) | copy-start | bytes 3145732
  7.2 3.5 %copy-start.13 = (bf16[512,512]{1,0:T(8,128)(2,1)S(1)}, bf16[512,512]{1,0:T(8,128)(2,1)}, u32[]{:S(2)}) copy-start(bf16[512,512]{1,0:T(8,128)(2,1)} %param.10) | copy-start | bytes 1572868
  7.2 131.1 %reduce-scatter.2.cloned.1.call-start = ((), (), s32[]{:S(2)}) async-start(), calls=%async_computation.3 | async-start | bytes 2949120 | tf_op jit(solution)/shard_map/reduce_scatter | solution.py:84
  13.5 1.1 copy-start.3
  14.9 5.0 %copy-start.5 = (bf16[512,256]{0,1:T(8,128)(2,1)}, bf16[512,256]{0,1:T(8,128)(2,1)S(1)}, u32[]{:S(2)}) copy-start(bf16[512,256]{0,1:T(8,128)(2,1)S(1)} %copy.45) | copy-start | bytes 786436
  15.0 4.8 %copy-start.7 = (bf16[512,256]{0,1:T(8,128)(2,1)}, bf16[512,256]{0,1:T(8,128)(2,1)S(1)}, u32[]{:S(2)}) copy-start(bf16[512,256]{0,1:T(8,128)(2,1)S(1)} %copy.43) | copy-start | bytes 786436
  19.9 1.3 copy-start.1
  21.2 1.1 copy-start.2
  25.7 4.9 %copy-start.8 = (bf16[512,256]{0,1:T(8,128)(2,1)S(1)}, bf16[512,256]{0,1:T(8,128)(2,1)}, u32[]{:S(2)}) copy-start(bf16[512,256]{0,1:T(8,128)(2,1)} %copy-done.7) | copy-start | bytes 786436
  27.6 2.9 %copy-start.11 = (bf16[512,256]{0,1:T(8,128)(2,1)}, bf16[512,256]{0,1:T(8,128)(2,1)S(1)}, u32[]{:S(2)}) copy-start(bf16[512,256]{0,1:T(8,128)(2,1)S(1)} %copy.48) | copy-start | bytes 786436
  27.6 2.9 %copy-start.12 = (f32[512,512]{1,0:T(8,128)S(1)}, f32[512,512]{1,0:T(8,128)}, u32[]{:S(2)}) copy-start(f32[512,512]{1,0:T(8,128)} %fusion.20) | copy-start | bytes 3145732
  30.5 4.2 %copy-start.6 = (bf16[512,256]{0,1:T(8,128)(2,1)S(1)}, bf16[512,256]{0,1:T(8,128)(2,1)}, u32[]{:S(2)}) copy-start(bf16[512,256]{0,1:T(8,128)(2,1)} %copy-done.5) | copy-start | bytes 786436
  35.5 3.5 %copy-start.9 = (bf16[4,64,512]{2,1,0:T(8,128)(2,1)S(1)}, bf16[4,64,512]{2,1,0:T(8,128)(2,1)}, u32[]{:S(2)}) copy-start(bf16[4,64,512]{2,1,0:T(8,128)(2,1)} %fusion.45) | copy-start | bytes 786436
  36.7 4.0 %copy-start.10 = (bf16[4,512,64]{1,2,0:T(8,128)(2,1)S(1)}, bf16[4,512,64]{1,2,0:T(8,128)(2,1)}, u32[]{:S(2)}) copy-start(bf16[4,512,64]{1,2,0:T(8,128)(2,1)} %fusion.43) | copy-start | bytes 786436
  44.2 1.0 copy-start.4
  47.0 0.7 copy-start.17
  47.0 0.9 copy-start.18
  49.0 13.8 %all-to-all-start = ((s32[8,1,256]{2,1,0:T(1,128)}), s32[8,1,256]{2,1,0:T(1,128)S(1)}, u32[]{:S(2)}, u32[]{:S(2)}) async-start(s32[8,1,256]{2,1,0:T(1,128)} %bitcast.1), calls=%async_computation | async-start | bytes 16384 | tf_op jit(solution)/shard_map/all_to_all | solution.py:120
  56.3 117.9 %all-reduce.3.cloned.1.call-start = ((), (), s32[]{:S(2)}) async-start(), calls=%async_computation.4 | async-start | bytes 1179648 | tf_op jit(solution)/shard_map/psum | solution.py:128
  57.6 1.1 copy-start.14
  133.1 45.4 %copy-start.19 = (f32[128]{0:T(128)S(1)}, f32[128]{0:T(128)}, u32[]{:S(2)}) copy-start(f32[128]{0:T(128)} %param.19) | copy-start | bytes 1540
  133.1 45.9 %copy-start.15 = (f32[128,512]{1,0:T(8,128)S(1)}, f32[128,512]{1,0:T(8,128)}, u32[]{:S(2)}) copy-start(f32[128,512]{1,0:T(8,128)} %param.18) | copy-start | bytes 786436
  133.1 45.9 %copy-start.16 = (f32[128,512]{1,0:T(8,128)S(1)}, f32[128,512]{1,0:T(8,128)}, u32[]{:S(2)}) copy-start(f32[128,512]{1,0:T(8,128)} %param.17) | copy-start | bytes 786436
Sparse Core Ops, SparseCore 0:
  47.1 91.1 reduce-scatter.1
  141.2 32.9 all-reduce.2
where the time goes:
time: 188 us
  blocking collectives  77.1 us (41%)
  waiting for transfers between devices  34.4 us (18%)
  matrix products  26 us (14%)
  other arithmetic  16.3 us (9%)
  between operations  14.3 us (8%)
  local copies, waits for them, and re-layouts  12.1 us (6%)
  starting transfers between devices  7.53 us (4%)
    all_to_all x1, blocking collectives, local(): lax.all_to_all(outgoing, 'rows', split_axis=0, concat_axis=0, tiled=True)  70.2 us
    psum x1, waiting for transfers between devices, local(): grad_all, count_all = lax.psum((grad_part, count_part), 'dp')  28.9 us
    dot_general x3, matrix products, core(): jnp.einsum('hts,shd->thd', weights, values_part, preferred_element_type=j...  7.85 us
    all_to_all x1, starting transfers between devices, local(): lax.all_to_all(out_slots, 'rows', split_axis=0, concat_axis=0, tiled=True)  7.28 us
    psum x1, blocking collectives, local(): grad_all, count_all = lax.psum((grad_part, count_part), 'dp')  6.85 us
    dot_general x3, matrix products, core(): jnp.einsum('thd,shd->hts', queries, keys_part, preferred_element_type=jnp...  6.76 us
    unnamed x42, local copies, waits for them, and re-layouts  4.69 us
    reduce_scatter x1, waiting for transfers between devices, local(): lax.psum_scatter(jnp.concatenate([lax.dot_general(normed, pre_grad_b, con...  4.02 us
  transfers between devices with their start and end apart: 3, of which 3 were waited for; matrix products, arithmetic and copies ran while one was open for 4% of the time, Pallas kernels for 0%

commit v1 on v0

--- a/solution.py
+++ b/solution.py
@@ -1,6 +1,10 @@
+import functools
+
 import jax
 import jax.numpy as jnp
 from jax import lax
+from jax.experimental import pallas as pl
+from jax.experimental.pallas import tpu as pltpu
 from jax.sharding import PartitionSpec as P
 
 HEADS = 4
@@ -26,7 +30,7 @@
 
 
 def allowed_mask(lengths, tok_count):
-    ends = jnp.cumsum(lengths)
+    ends = jnp.stack([jnp.sum(lengths[: i + 1]) for i in range(lengths.shape[0])])
     position = jnp.arange(tok_count, dtype=jnp.int32)
     segment = jnp.sum((position[:, None] >= ends[None, :]).astype(jnp.int32), axis=1)
     same = segment[:, None] == segment[None, :]
@@ -130,6 +134,321 @@
     return (new_rows, new_mom, new_var, w_in_grad, w_out_grad)
 
 
+BF16 = jnp.bfloat16
+F32 = jnp.float32
+
+AXES = {"core": ("dp", 1), "x": ("dp", 2), "y": ("rows", 1), "z1": ("rows", 2), "z2": ("rows", 4)}
+
+
+class Part:
+    def __init__(self, name, owner_rows, cols, halve, swap):
+        self.name, self.cols, self.halve, self.swap = name, cols, halve, swap
+        self.gather = [a for a in halve if AXES[a][0] == "dp"][::-1]
+        self.height = owner_rows // 2 ** len(self.gather)
+        self.stages = [("halve", a) for a in halve] + [("swap", a) for a in swap]
+        self.stages += [("gather", a) for a in self.gather]
+
+    def shapes(self):
+        chunk = (self.height, self.cols)
+        halves = len(self.halve)
+        shapes = [(2,) * halves + chunk]
+        for step in range(halves):
+            shapes.append((2,) * (halves - step - 1) + chunk)
+        shapes += [chunk] * len(self.swap)
+        gathered = [(2,) * (k + 1) + chunk for k in range(len(self.gather))]
+        arrive = [(2,) * (halves - step - 1) + chunk for step in range(halves)] + [chunk] * len(self.swap)
+        return shapes + gathered, arrive
+
+
+class Exchange:
+    def __init__(self, part, bufs, arrive, send_sems, recv_sems, base, bit, peer):
+        self.part, self.bufs, self.arrive = part, bufs, arrive
+        self.send_sems, self.recv_sems, self.base = send_sems, recv_sems, base
+        self.bit, self.peer = bit, peer
+        self.stage, self.copy = 0, None
+
+    def put(self, owner, inner, value):
+        bits = {"y": owner % 2, "z1": owner // 2 % 2, "z2": owner // 4, **inner}
+        self.bufs[0][tuple(bits[a] for a in self.part.halve)] = value
+
+    def put_rows(self, value):
+        dims, height = self.part.gather[::-1], self.part.height
+        per_owner = height * 2 ** len(dims)
+        for owner in range(8):
+            for q in range(2 ** len(dims)):
+                inner = {a: q // 2 ** (len(dims) - 1 - k) % 2 for k, a in enumerate(dims)}
+                first = owner * per_owner + q * height
+                self.put(owner, inner, value[first : first + height].astype(BF16))
+
+    def start(self):
+        kind, axis = self.part.stages[self.stage]
+        here = self.bufs[self.stage]
+        if kind == "halve":
+            source, target = here.at[1 - self.bit[axis]], self.arrive[self.stage]
+        elif kind == "swap":
+            source, target = here, self.arrive[self.stage]
+        else:
+            later = self.bufs[self.stage + 1]
+            later[self.bit[axis]] = here[...]
+            source = target = later.at[self.bit[axis]]
+        self.copy = pltpu.make_async_remote_copy(
+            src_ref=source,
+            dst_ref=target,
+            send_sem=self.send_sems.at[self.base + self.stage],
+            recv_sem=self.recv_sems.at[self.base + self.stage],
+            device_id=self.peer[axis],
+            device_id_type=pl.DeviceIdType.MESH,
+        )
+        self.copy.start()
+
+    def step(self):
+        if self.stage == len(self.part.stages):
+            return
+        kind, axis = self.part.stages[self.stage]
+        self.copy.wait()
+        if kind != "gather":
+            mine = self.bufs[self.stage][self.bit[axis]] if kind == "halve" else self.bufs[self.stage][...]
+            total = mine.astype(F32) + self.arrive[self.stage][...].astype(F32)
+            self.bufs[self.stage + 1][...] = total.astype(BF16)
+        self.stage += 1
+        if self.stage < len(self.part.stages):
+            self.start()
+
+    def result(self):
+        out = self.bufs[-1][...]
+        return out.reshape(-1, self.part.cols).astype(F32)
+
+
+def dot(a, b, dims=((1,), (0,))):
+    return lax.dot_general(a, b, (dims, ((), ())), preferred_element_type=F32)
+
+
+def norm_parts(values):
+    average = jnp.mean(values, axis=-1, keepdims=True)
+    centered = values - average
+    spread = jnp.mean(centered * centered, axis=-1, keepdims=True)
+    scale = lax.rsqrt(spread + norm_eps)
+    return centered * scale, scale
+
+
+def norm_back(grad, normed, scale):
+    inner = jnp.mean(grad * normed, axis=-1, keepdims=True)
+    return scale * (grad - jnp.mean(grad, axis=-1, keepdims=True) - normed * inner)
+
+
+def sigmoid(values):
+    return 0.5 * jnp.tanh(0.5 * values) + 0.5
+
+
+def column_of(row, count):
+    return jnp.broadcast_to(row, (count, count)).T[:, :1]
+
+
+def parts_of(slots, w_rows):
+    return [
+        Part("count", 16, slots, ["y", "z1", "z2"], ["x", "core"]),
+        Part("early", w_rows, 3 * HW, ["core", "y", "z1", "z2"], ["x"]),
+        Part("late", w_rows, 2 * HW, ["core", "x", "z1", "z2", "y"], []),
+        Part("rows_a", slots, 256, ["core", "y", "z1", "z2"], ["x"]),
+        Part("rows_b", slots, 256, ["core", "x", "z1", "z2", "y"], []),
+    ]
+
+
+def fused_kernel(parts, lens, tokens, grads, index, w_in, w_out, rows, mom, var, *rest):
+    new_rows, new_mom, new_var, w_in_out, w_out_out = rest[:5]
+    rest = list(rest[5:])
+    send_sems, recv_sems, normed_t, slope, wst, dst, fac = rest[:7]
+    rest = rest[7:]
+    tok, width = tokens.shape
+    slots = rows.shape[0]
+    owners = 8
+    r, p = lax.axis_index("rows"), lax.axis_index("dp")
+    bit, peer = {}, {}
+    for axis, (name, unit) in AXES.items():
+        at = r if name == "rows" else p
+        bit[axis] = at // unit % 2
+        other = at + unit - 2 * unit * bit[axis]
+        peer[axis] = (other, p) if name == "rows" else (r, other)
+    barrier = pltpu.get_barrier_semaphore()
+    for axis in AXES:
+        pl.semaphore_signal(barrier, inc=1, device_id=peer[axis], device_id_type=pl.DeviceIdType.MESH)
+    pl.semaphore_wait(barrier, len(AXES))
+
+    made, base = {}, 0
+    for part in parts:
+        shapes, arrive = part.shapes()
+        bufs = [rest.pop(0) for _ in shapes]
+        landing = [rest.pop(0) for _ in arrive]
+        made[part.name] = Exchange(part, bufs, landing, send_sems, recv_sems, base, bit, peer)
+        base += len(part.stages)
+    count, early, late = made["count"], made["early"], made["late"]
+    rows_a, rows_b = made["rows_a"], made["rows_b"]
+
+    row_id = lax.broadcasted_iota(jnp.int32, (owners * slots, tok), 0)
+    named = (row_id == index[...]).astype(F32).astype(BF16)
+    counts = dot(jnp.ones((16, tok), BF16), named, ((1,), (1,)))
+    for owner in range(owners):
+        count.put(owner, {}, counts[:, owner * slots : (owner + 1) * slots].astype(BF16))
+    count.start()
+
+    exact, scale_in = norm_parts(tokens[...].astype(F32))
+    normed = exact.astype(BF16)
+    normed_t[...] = normed.T
+    proj = []
+    for k in range(4):
+        pre = dot(normed, w_in[:, k * HW : (k + 1) * HW])
+        gate = sigmoid(pre)
+        proj.append((pre * gate).astype(BF16))
+        slope[:, k * HW : (k + 1) * HW] = gate * (1.0 + pre * (1.0 - gate))
+    upart, vpart, qpart, kpart = proj
+    count.step()
+
+    feature = lax.broadcasted_iota(jnp.int32, (1, HW), 1) // HEAD_DIM
+    heads = [(feature == h).astype(F32).astype(BF16) for h in range(HEADS)]
+    block = MAXLEN // 2
+    spans = [(i * block, max(0, i - 2) * block, (i + 1) * block) for i in range(tok // block)]
+    ends, total = [], 0
+    for s in range(lens.shape[1]):
+        total = total + lens[0, s]
+        ends.append(total)
+
+    def segment(position):
+        return sum((position >= e).astype(jnp.int32) for e in ends)
+
+    masks = []
+    for at, low, high in spans:
+        query = at + lax.broadcasted_iota(jnp.int32, (block, 1), 0)
+        key = low + lax.broadcasted_iota(jnp.int32, (1, high - low), 1)
+        masks.append((segment(query) == segment(key)) & (key <= query))
+    attn_rows = [None] * len(spans)
+    for h in range(HEADS):
+        keys, vals = kpart * heads[h], vpart * heads[h]
+        for i, (at, low, high) in enumerate(spans):
+            scores = dot(qpart[at : at + block], keys[low:high], ((1,), (1,))) * HEAD_DIM ** (-0.5)
+            gate = jnp.where(masks[i], sigmoid(scores), 0.0)
+            mass = (scores * gate * (1.0 / MAXLEN)).astype(BF16)
+            here = pl.ds(h * tok + at, block)
+            if low > 0:
+                wst[here, 0:low] = jnp.zeros((block, low), BF16)
+                dst[here, 0:low] = jnp.zeros((block, low), BF16)
+            if high < tok:
+                wst[here, high:tok] = jnp.zeros((block, tok - high), BF16)
+                dst[here, high:tok] = jnp.zeros((block, tok - high), BF16)
+            wst[here, low:high] = mass
+            fac[here, low:high] = gate * (1.0 + scores * (1.0 - sigmoid(scores))) * (HEAD_DIM ** (-0.5) / MAXLEN)
+            piece = dot(mass, vals[low:high])
+            attn_rows[i] = piece if attn_rows[i] is None else attn_rows[i] + piece
+        count.step()
+    attn_hat, scale_mid = norm_parts(jnp.concatenate(attn_rows, axis=0))
+    gate_u = upart.astype(F32)
+    y_out = (attn_hat * gate_u).astype(BF16)
+
+    y_grad = dot(grads[...], w_out[...]).astype(BF16).astype(F32)
+    u_grad = (y_grad * attn_hat).astype(BF16).astype(F32)
+    attn_grad = norm_back(y_grad * gate_u, attn_hat, scale_mid).astype(BF16)
+    v_grad = 0.0
+    for h in range(HEADS):
+        v_grad = v_grad + dot(wst[h * tok : (h + 1) * tok, :], attn_grad * heads[h], ((0,), (0,)))
+    pre_u = (u_grad * slope[:, :HW]).astype(BF16)
+    pre_v = (v_grad.astype(BF16).astype(F32) * slope[:, HW : 2 * HW]).astype(BF16)
+    early.put_rows(
+        jnp.concatenate(
+            [dot(grads[...].T, y_out), dot(normed_t[...], pre_u), dot(normed_t[...], pre_v)], axis=1
+        )
+    )
+    early.start()
+    q_rows = [None] * len(spans)
+    k_grad = 0.0
+    for h in range(HEADS):
+        keys, vals, queries = kpart * heads[h], vpart * heads[h], qpart * heads[h]
+        for i, (at, low, high) in enumerate(spans):
+            here = pl.ds(h * tok + at, block)
+            mass_grad = dot(attn_grad[at : at + block], vals[low:high], ((1,), (1,)))
+            score_grad = (mass_grad.astype(BF16).astype(F32) * fac[here, low:high]).astype(BF16)
+            dst[here, low:high] = score_grad
+            piece = dot(score_grad, keys[low:high])
+            q_rows[i] = piece if q_rows[i] is None else q_rows[i] + piece
+        k_grad = k_grad + dot(dst[h * tok : (h + 1) * tok, :], queries, ((0,), (0,)))
+        if h % 2 == 1:
+            early.step()
+    q_grad = jnp.concatenate(q_rows, axis=0)
+    pre_q = (q_grad.astype(BF16).astype(F32) * slope[:, 2 * HW : 3 * HW]).astype(BF16)
+    pre_k = (k_grad.astype(BF16).astype(F32) * slope[:, 3 * HW :]).astype(BF16)
+
+    normed_grad = 0.0
+    for k, piece in enumerate((pre_u, pre_v, pre_q, pre_k)):
+        normed_grad = normed_grad + dot(piece, w_in[:, k * HW : (k + 1) * HW], ((1,), (1,)))
+    exact, scale_in = norm_parts(tokens[...].astype(F32))
+    emb_grad = (norm_back(normed_grad, exact, scale_in) + grads[...].astype(F32)).astype(BF16)
+    rows_a.put_rows(dot(named, emb_grad[:, :256]))
+    rows_a.start()
+    rows_b.put_rows(dot(named, emb_grad[:, 256:]))
+    rows_b.start()
+    late.put_rows(jnp.concatenate([dot(normed_t[...], pre_q), dot(normed_t[...], pre_k)], axis=1))
+    late.start()
+    for _ in range(8):
+        for exchange in (rows_a, rows_b, early, late, count):
+            exchange.step()
+
+    grad_a, grad_b = rows_a.result(), rows_b.result()
+    touched = column_of(count.result()[:1], slots) > 0.5
+    squares = jnp.sum(grad_a * grad_a, axis=1, keepdims=True) + jnp.sum(grad_b * grad_b, axis=1, keepdims=True)
+    var_now = column_of(var[...], slots)
+    var_next = beta_two * var_now + (1.0 - beta_two) * (squares * (1.0 / width))
+    divisor = jnp.sqrt(var_next / bias_two) + adam_eps
+    for at, grad in ((0, grad_a), (256, grad_b)):
+        cols = slice(at, at + 256)
+        mom_next = beta_one * mom[:, cols] + (1.0 - beta_one) * grad
+        rows_next = rows[:, cols] - learn_rate * (mom_next / bias_one / divisor)
+        new_rows[:, cols] = jnp.where(touched, rows_next, rows[:, cols])
+        new_mom[:, cols] = jnp.where(touched, mom_next, mom[:, cols])
+    var_out = jnp.where(touched, var_next, var_now)
+    new_var[...] = jnp.broadcast_to(var_out, (slots, slots)).T[:1]
+    out_early = early.result()
+    w_out_out[...] = out_early[:, :HW]
+    w_in_out[:, : 2 * HW] = out_early[:, HW:]
+    w_in_out[:, 2 * HW :] = late.result()
+
+
+def fused(tokens, out_grad, seq_lengths, owners, slots, w_in, w_out, emb_rows, emb_mom, emb_var):
+    tok, width = tokens.shape
+    count = emb_rows.shape[0]
+    w_rows = w_in.shape[0] // lax.axis_size("rows")
+    index = (owners.reshape(1, tok) * count + slots.reshape(1, tok)).astype(jnp.int32)
+    parts = parts_of(count, w_rows)
+    stages = sum(len(part.stages) for part in parts)
+    scratch = [
+        pltpu.SemaphoreType.DMA((stages,)),
+        pltpu.SemaphoreType.DMA((stages,)),
+        pltpu.VMEM((width, tok), BF16),
+        pltpu.VMEM((tok, 4 * HW), F32),
+        pltpu.VMEM((HEADS * tok, tok), BF16),
+        pltpu.VMEM((HEADS * tok, tok), BF16),
+        pltpu.VMEM((HEADS * tok, tok), F32),
+    ]
+    for part in parts:
+        shapes, arrive = part.shapes()
+        scratch += [pltpu.VMEM(shape, BF16) for shape in shapes + arrive]
+    vmem = pl.BlockSpec(memory_space=pltpu.VMEM)
+    new_rows, new_mom, new_var, w_in_grad, w_out_grad = pl.pallas_call(
+        functools.partial(fused_kernel, parts),
+        out_shape=(
+            jax.ShapeDtypeStruct(emb_rows.shape, F32),
+            jax.ShapeDtypeStruct(emb_mom.shape, F32),
+            jax.ShapeDtypeStruct((1, count), F32),
+            jax.ShapeDtypeStruct((w_rows, w_in.shape[1]), F32),
+            jax.ShapeDtypeStruct((w_rows, w_out.shape[1]), F32),
+        ),
+        in_specs=[pl.BlockSpec(memory_space=pltpu.SMEM)] + [vmem] * 8,
+        out_specs=[vmem] * 5,
+        scratch_shapes=scratch,
+        compiler_params=pltpu.CompilerParams(
+            collective_id=0, has_side_effects=True, vmem_limit_bytes=56 * 2**20
+        ),
+    )(seq_lengths, tokens, out_grad, index, w_in, w_out, emb_rows, emb_mom, emb_var.reshape(1, count))
+    return new_rows, new_mom, new_var.reshape(count), w_in_grad, w_out_grad
+
+
 def solution(mesh):
     in_specs = (
         P(("rows", "dp"), None),
@@ -144,4 +463,5 @@
         P("rows"),
     )
     out_specs = (P("rows", None), P("rows", None), P("rows"), P("rows", None), P("rows", None))
-    return jax.shard_map(local, mesh=mesh, in_specs=in_specs, out_specs=out_specs, check_vma=False)
+    small = mesh.shape["rows"] == 8 and mesh.shape["dp"] == 4
+    return jax.shard_map(fused if small else local, mesh=mesh, in_specs=in_specs, out_specs=out_specs, check_vma=False)

time: 188 us -> 63.2 us (0.34)
  blocking collectives: 77.1 us -> 0 us
  Pallas kernels: 0 us -> 56.6 us
  waiting for transfers between devices: 34.4 us -> 0 us
  matrix products: 26 us -> 0 us
  other arithmetic: 16.3 us -> 1.27 us
  between operations: 14.3 us -> 0.66 us
  local copies, waits for them, and re-layouts: 12.1 us -> 4.43 us
  starting transfers between devices: 7.53 us -> 0 us
    all_to_all x1 -> x0, blocking collectives: 70.2 us -> none  [local(): lax.all_to_all(outgoing, 'rows', split_axis=0, concat_axis=0, tiled=True)]
    pallas_call x0 -> x1, Pallas kernels: none -> 56.6 us  [fused(): pl.pallas_call(functools.partial(fused_kernel, parts), out_shape=(jax.Sha...]
    psum x1 -> x0, waiting for transfers between devices: 28.9 us -> none  [local(): grad_all, count_all = lax.psum((grad_part, count_part), 'dp')]
    dot_general x13 -> x0, matrix products: 26 us -> none  [the longest x3 7.85 us: core(): jnp.einsum('hts,shd->thd', weights, values_part, preferred_element_type=j...]
    all_to_all x1 -> x0, starting transfers between devices: 7.28 us -> none  [local(): lax.all_to_all(out_slots, 'rows', split_axis=0, concat_axis=0, tiled=True)]
    psum x1 -> x0, blocking collectives: 6.85 us -> none  [local(): grad_all, count_all = lax.psum((grad_part, count_part), 'dp')]
    reduce_sum x10 -> x0, other arithmetic: 4.7 us -> none  [the longest x2 2.22 us: layer_norm(): centered = values - average]
    reduce_scatter x1 -> x0, waiting for transfers between devices: 4.02 us -> none  [local(): lax.psum_scatter(jnp.concatenate([lax.dot_general(normed, pre_grad_b, con...]
  transfers between devices with their start and end apart: 3 -> 0, of which waited for: 3 -> 0; matrix products, arithmetic and copies ran while one was open for 4% -> 0% of each run, Pallas kernels for 0% -> 0%
where the time goes in v1:
time: 63.2 us; the launch traced here: 62.9 us
  Pallas kernels  56.6 us (90%)
  local copies, waits for them, and re-layouts  4.43 us (7%)
  other arithmetic  1.27 us (2%)
  between operations  0.66 us (1%)
    pallas_call x1, Pallas kernels, fused(): pl.pallas_call(functools.partial(fused_kernel, parts), out_shape=(jax.Sha...  56.6 us
    unnamed x15, local copies, waits for them, and re-layouts  4.43 us

profile of v1, /device:TPU:0, one launch (start us, length us, event | category | flops | bytes accessed | tf_op | source)
XLA Modules:
  0.0 62.9 jit_solution(9242580169293943569)
XLA Ops:
  0.6 0.0 copy-start.3
  0.6 0.7 %broadcast_multiply_fusion = s32[512,1]{0,1:T(1,128)S(1)} fusion(s32[512,1]{0,1:T(1,128)} %param.13), kind=kLoop, calls=%fused_computation | loop fusion | flops 512 | bytes 4096 | tf_op jit(solution)/shard_map/mul | solution.py:417
  1.3 0.0 copy-done.3
  1.3 0.6 add.5
  1.9 56.6 %shard_map.137 = (f32[128,512]{1,0:T(8,128)}, f32[128,512]{1,0:T(8,128)}, f32[1,128]{1,0:T(1,128)}, f32[64,1024]{1,0:T(8,128)}, f32[64,256]{1,0:T(8,128)}) custom-call(s32[1,4]{1,0:T(1,128)} %lens.1, bf16[512,512]{1,0:T(8,128)(2,1)} %tokens.1, bf16[512,512]{1,0:T(8,128)(2,1)} %grads.1, s32[1,512]{1,0:T(1,128)} %bitcast.4, bf16[512,1024]{1,0:T(8,128)(2,1)} %w_in.1, ...), custom_call_target="tpu_custom_call" | custom-call | tf_op jit(solution)/shard_map/pallas_call | solution.py:433
  58.5 0.0 copy-start.1
  58.5 1.7 %copy.20 = f32[128,512]{1,0:T(8,128)} copy(f32[128,512]{1,0:T(8,128)} %get-tuple-element.20) | data formatting | bytes 524288
  60.2 0.0 copy-done.1
  60.2 0.0 copy-start.4
  60.2 0.0 copy-start
  60.2 0.7 %copy.21 = f32[128,512]{1,0:T(8,128)} copy(f32[128,512]{1,0:T(8,128)S(1)} %copy-done.1) | data formatting | bytes 524288
  60.9 0.0 copy-done.4
  60.9 0.5 copy.22
  61.4 0.0 copy-done
  61.4 0.0 copy-start.2
  61.4 0.7 %copy.23 = f32[64,1024]{1,0:T(8,128)} copy(f32[64,1024]{1,0:T(8,128)S(1)} %copy-done) | data formatting | bytes 524288
  62.1 0.2 copy-done.2
  62.3 0.6 copy.24
Async XLA Ops:
  0.6 0.7 %copy-start.3 = (s32[512]{0:T(512)S(1)}, s32[512]{0:T(512)}, u32[]{:S(2)}) copy-start(s32[512]{0:T(512)} %param.14) | copy-start | bytes 6148
  58.5 1.7 %copy-start.1 = (f32[128,512]{1,0:T(8,128)S(1)}, f32[128,512]{1,0:T(8,128)}, u32[]{:S(2)}) copy-start(f32[128,512]{1,0:T(8,128)} %get-tuple-element.21) | copy-start | bytes 786436
  60.2 0.7 %copy-start.4 = (f32[1,128]{1,0:T(1,128)S(1)}, f32[1,128]{1,0:T(1,128)}, u32[]{:S(2)}) copy-start(f32[1,128]{1,0:T(1,128)} %get-tuple-element.12) | copy-start | bytes 1540
  60.2 1.2 %copy-start = (f32[64,1024]{1,0:T(8,128)S(1)}, f32[64,1024]{1,0:T(8,128)}, u32[]{:S(2)}) copy-start(f32[64,1024]{1,0:T(8,128)} %get-tuple-element.23) | copy-start | bytes 786436
  61.4 0.9 %copy-start.2 = (f32[64,256]{1,0:T(8,128)S(1)}, f32[64,256]{1,0:T(8,128)}, u32[]{:S(2)}) copy-start(f32[64,256]{1,0:T(8,128)} %get-tuple-element.24) | copy-start | bytes 196612

commit v2 on v1

--- a/solution.py
+++ b/solution.py
@@ -137,86 +137,95 @@
 BF16 = jnp.bfloat16
 F32 = jnp.float32
 
-AXES = {"core": ("dp", 1), "x": ("dp", 2), "y": ("rows", 1), "z1": ("rows", 2), "z2": ("rows", 4)}
+CUTS = {"core": 2, "x": 2, "y": 2, "z": 4, "rows": 8}
 
 
 class Part:
-    def __init__(self, name, owner_rows, cols, halve, swap):
-        self.name, self.cols, self.halve, self.swap = name, cols, halve, swap
-        self.gather = [a for a in halve if AXES[a][0] == "dp"][::-1]
-        self.height = owner_rows // 2 ** len(self.gather)
-        self.stages = [("halve", a) for a in halve] + [("swap", a) for a in swap]
-        self.stages += [("gather", a) for a in self.gather]
+    def __init__(self, name, owner_rows, cols, cuts, last):
+        self.name, self.cols, self.cuts, self.last = name, cols, cuts, last
+        self.inner = [c for c in cuts if c in ("core", "x")]
+        self.height = owner_rows // 2 ** len(self.inner)
+        self.moves = [CUTS[c] - 1 for c in cuts] + [3]
 
     def shapes(self):
         chunk = (self.height, self.cols)
-        halves = len(self.halve)
-        shapes = [(2,) * halves + chunk]
-        for step in range(halves):
-            shapes.append((2,) * (halves - step - 1) + chunk)
-        shapes += [chunk] * len(self.swap)
-        gathered = [(2,) * (k + 1) + chunk for k in range(len(self.gather))]
-        arrive = [(2,) * (halves - step - 1) + chunk for step in range(halves)] + [chunk] * len(self.swap)
-        return shapes + gathered, arrive
+        sizes = [CUTS[c] for c in self.cuts]
+        bufs = [tuple(sizes[k:]) + chunk for k in range(len(sizes) + 1)]
+        arrive = [(n - 1,) + bufs[k + 1] for k, n in enumerate(sizes)]
+        last = (4,) + chunk if self.last == "gather" else (3,) + chunk
+        return bufs, arrive + [last]
 
 
 class Exchange:
-    def __init__(self, part, bufs, arrive, send_sems, recv_sems, base, bit, peer):
+    def __init__(self, part, bufs, arrive, send_sems, recv_sems, base, place):
         self.part, self.bufs, self.arrive = part, bufs, arrive
         self.send_sems, self.recv_sems, self.base = send_sems, recv_sems, base
-        self.bit, self.peer = bit, peer
-        self.stage, self.copy = 0, None
+        self.place, self.stage, self.copies = place, 0, []
 
     def put(self, owner, inner, value):
-        bits = {"y": owner % 2, "z1": owner // 2 % 2, "z2": owner // 4, **inner}
-        self.bufs[0][tuple(bits[a] for a in self.part.halve)] = value
+        at = {"y": owner % 2, "z": owner // 2, "rows": owner, **inner}
+        self.bufs[0][tuple(at[c] for c in self.part.cuts)] = value
 
     def put_rows(self, value):
-        dims, height = self.part.gather[::-1], self.part.height
-        per_owner = height * 2 ** len(dims)
+        names, height = self.part.inner, self.part.height
+        per_owner = height * 2 ** len(names)
         for owner in range(8):
-            for q in range(2 ** len(dims)):
-                inner = {a: q // 2 ** (len(dims) - 1 - k) % 2 for k, a in enumerate(dims)}
+            for q in range(2 ** len(names)):
+                inner = {c: q // 2 ** (len(names) - 1 - k) % 2 for k, c in enumerate(names)}
                 first = owner * per_owner + q * height
                 self.put(owner, inner, value[first : first + height].astype(BF16))
 
     def start(self):
-        kind, axis = self.part.stages[self.stage]
-        here = self.bufs[self.stage]
-        if kind == "halve":
-            source, target = here.at[1 - self.bit[axis]], self.arrive[self.stage]
-        elif kind == "swap":
-            source, target = here, self.arrive[self.stage]
+        here, landing = self.bufs[self.stage], self.arrive[self.stage]
+        self.copies = []
+        if self.stage < len(self.part.cuts):
+            at, takers = self.place[self.part.cuts[self.stage]]
+            moves = [(here.at[where], landing.at[k], device) for k, (where, device) in enumerate(takers)]
         else:
-            later = self.bufs[self.stage + 1]
-            later[self.bit[axis]] = here[...]
-            source = target = later.at[self.bit[axis]]
-        self.copy = pltpu.make_async_remote_copy(
-            src_ref=source,
-            dst_ref=target,
-            send_sem=self.send_sems.at[self.base + self.stage],
-            recv_sem=self.recv_sems.at[self.base + self.stage],
-            device_id=self.peer[axis],
-            device_id_type=pl.DeviceIdType.MESH,
-        )
-        self.copy.start()
+            block, peers = self.place["dp"]
+            if self.part.last == "gather":
+                landing[block] = here[...]
+                moves = [(landing.at[block], landing.at[block], device) for device in peers]
+            else:
+                moves = [(here, landing.at[k], device) for k, device in enumerate(peers)]
+        for k, (source, target, device) in enumerate(moves):
+            copy = pltpu.make_async_remote_copy(
+                src_ref=source,
+                dst_ref=target,
+                send_sem=self.send_sems.at[self.base + k],
+                recv_sem=self.recv_sems.at[self.base + k],
+                device_id=device,
+                device_id_type=pl.DeviceIdType.MESH,
+            )
+            copy.start()
+            self.copies.append(copy)
 
     def step(self):
-        if self.stage == len(self.part.stages):
+        if self.stage == len(self.part.moves):
             return
-        kind, axis = self.part.stages[self.stage]
-        self.copy.wait()
-        if kind != "gather":
-            mine = self.bufs[self.stage][self.bit[axis]] if kind == "halve" else self.bufs[self.stage][...]
-            total = mine.astype(F32) + self.arrive[self.stage][...].astype(F32)
+        for copy in self.copies:
+            copy.wait()
+        if self.stage < len(self.part.cuts):
+            at, _ = self.place[self.part.cuts[self.stage]]
+            total = self.bufs[self.stage][at].astype(F32)
+            for k in range(self.part.moves[self.stage]):
+                total = total + self.arrive[self.stage][k].astype(F32)
             self.bufs[self.stage + 1][...] = total.astype(BF16)
+        self.base += self.part.moves[self.stage]
         self.stage += 1
-        if self.stage < len(self.part.stages):
+        if self.stage < len(self.part.moves):
             self.start()
 
     def result(self):
-        out = self.bufs[-1][...]
-        return out.reshape(-1, self.part.cols).astype(F32)
+        here, landing = self.bufs[-1], self.arrive[-1]
+        if self.part.last == "gather":
+            return landing[...].reshape(-1, self.part.cols).astype(F32)
+        by_core, by_x, by_both = (landing[k].astype(F32) for k in range(3))
+        mine, other = here[...].astype(F32) + by_x, by_core + by_both
+        if self.part.last == "sum":
+            return mine + other
+        first = self.place["core"][0] == 0
+        return jnp.concatenate([jnp.where(first, mine, other), jnp.where(first, other, mine)], axis=0)
 
 
 def dot(a, b, dims=((1,), (0,))):
@@ -246,11 +255,11 @@
 
 def parts_of(slots, w_rows):
     return [
-        Part("count", 16, slots, ["y", "z1", "z2"], ["x", "core"]),
-        Part("early", w_rows, 3 * HW, ["core", "y", "z1", "z2"], ["x"]),
-        Part("late", w_rows, 2 * HW, ["core", "x", "z1", "z2", "y"], []),
-        Part("rows_a", slots, 256, ["core", "y", "z1", "z2"], ["x"]),
-        Part("rows_b", slots, 256, ["core", "x", "z1", "z2", "y"], []),
+        Part("count", 16, slots, ["y", "z"], "sum"),
+        Part("early", w_rows, 3 * HW, ["core", "x", "rows"], "gather"),
+        Part("late", w_rows, 2 * HW, ["core", "y", "z"], "pair"),
+        Part("rows_a", slots, 256, ["core", "y", "z"], "pair"),
+        Part("rows_b", slots, 256, ["core", "x", "rows"], "gather"),
     ]
 
 
@@ -263,24 +272,31 @@
     slots = rows.shape[0]
     owners = 8
     r, p = lax.axis_index("rows"), lax.axis_index("dp")
-    bit, peer = {}, {}
-    for axis, (name, unit) in AXES.items():
-        at = r if name == "rows" else p
-        bit[axis] = at // unit % 2
-        other = at + unit - 2 * unit * bit[axis]
-        peer[axis] = (other, p) if name == "rows" else (r, other)
+    core, x, y, z = p % 2, p // 2, r % 2, r // 2
+    by_core, by_x = (r, p + 1 - 2 * core), (r, p + 2 - 4 * x)
+    by_both, by_y = (r, 3 - p), (r + 1 - 2 * y, p)
+    by_rows = [lax.rem(r + k, owners) for k in range(1, owners)]
+    place = {
+        "core": (core, [(1 - core, by_core)]),
+        "x": (x, [(1 - x, by_x)]),
+        "y": (y, [(1 - y, by_y)]),
+        "z": (z, [(by_rows[2 * k - 1] // 2, (by_rows[2 * k - 1], p)) for k in (1, 2, 3)]),
+        "rows": (r, [(to, (to, p)) for to in by_rows]),
+        "dp": (core * 2 + x, [by_core, by_x, by_both]),
+    }
     barrier = pltpu.get_barrier_semaphore()
-    for axis in AXES:
-        pl.semaphore_signal(barrier, inc=1, device_id=peer[axis], device_id_type=pl.DeviceIdType.MESH)
-    pl.semaphore_wait(barrier, len(AXES))
+    greeted = [by_core, by_x, by_both] + [(to, p) for to in by_rows]
+    for device in greeted:
+        pl.semaphore_signal(barrier, inc=1, device_id=device, device_id_type=pl.DeviceIdType.MESH)
+    pl.semaphore_wait(barrier, len(greeted))
 
     made, base = {}, 0
     for part in parts:
         shapes, arrive = part.shapes()
         bufs = [rest.pop(0) for _ in shapes]
         landing = [rest.pop(0) for _ in arrive]
-        made[part.name] = Exchange(part, bufs, landing, send_sems, recv_sems, base, bit, peer)
-        base += len(part.stages)
+        made[part.name] = Exchange(part, bufs, landing, send_sems, recv_sems, base, place)
+        base += sum(part.moves)
     count, early, late = made["count"], made["early"], made["late"]
     rows_a, rows_b = made["rows_a"], made["rows_b"]
 
@@ -301,7 +317,6 @@
         proj.append((pre * gate).astype(BF16))
         slope[:, k * HW : (k + 1) * HW] = gate * (1.0 + pre * (1.0 - gate))
     upart, vpart, qpart, kpart = proj
-    count.step()
 
     feature = lax.broadcasted_iota(jnp.int32, (1, HW), 1) // HEAD_DIM
     heads = [(feature == h).astype(F32).astype(BF16) for h in range(HEADS)]
@@ -338,7 +353,6 @@
             fac[here, low:high] = gate * (1.0 + scores * (1.0 - sigmoid(scores))) * (HEAD_DIM ** (-0.5) / MAXLEN)
             piece = dot(mass, vals[low:high])
             attn_rows[i] = piece if attn_rows[i] is None else attn_rows[i] + piece
-        count.step()
     attn_hat, scale_mid = norm_parts(jnp.concatenate(attn_rows, axis=0))
     gate_u = upart.astype(F32)
     y_out = (attn_hat * gate_u).astype(BF16)
@@ -371,6 +385,7 @@
         k_grad = k_grad + dot(dst[h * tok : (h + 1) * tok, :], queries, ((0,), (0,)))
         if h % 2 == 1:
             early.step()
+            count.step()
     q_grad = jnp.concatenate(q_rows, axis=0)
     pre_q = (q_grad.astype(BF16).astype(F32) * slope[:, 2 * HW : 3 * HW]).astype(BF16)
     pre_k = (k_grad.astype(BF16).astype(F32) * slope[:, 3 * HW :]).astype(BF16)
@@ -386,8 +401,8 @@
     rows_b.start()
     late.put_rows(jnp.concatenate([dot(normed_t[...], pre_q), dot(normed_t[...], pre_k)], axis=1))
     late.start()
-    for _ in range(8):
-        for exchange in (rows_a, rows_b, early, late, count):
+    for _ in range(4):
+        for exchange in (early, rows_a, rows_b, late, count):
             exchange.step()
 
     grad_a, grad_b = rows_a.result(), rows_b.result()
@@ -416,7 +431,7 @@
     w_rows = w_in.shape[0] // lax.axis_size("rows")
     index = (owners.reshape(1, tok) * count + slots.reshape(1, tok)).astype(jnp.int32)
     parts = parts_of(count, w_rows)
-    stages = sum(len(part.stages) for part in parts)
+    stages = sum(sum(part.moves) for part in parts)
     scratch = [
         pltpu.SemaphoreType.DMA((stages,)),
         pltpu.SemaphoreType.DMA((stages,)),

time: 63.2 us -> 51.9 us (0.82)
  Pallas kernels: 56.6 us -> 45.3 us
    pallas_call x1, Pallas kernels: 56.6 us -> 45.3 us  [fused(): pl.pallas_call(functools.partial(fused_kernel, parts), out_shape=(jax.Sha...]
where the time goes in v2:
time: 51.9 us; the launch traced here: 51.7 us
  Pallas kernels  45.3 us (87%)
  local copies, waits for them, and re-layouts  4.43 us (9%)
  other arithmetic  1.27 us (2%)
  between operations  0.66 us (1%)
    pallas_call x1, Pallas kernels, fused(): pl.pallas_call(functools.partial(fused_kernel, parts), out_shape=(jax.Sha...  45.3 us
    unnamed x15, local copies, waits for them, and re-layouts  4.43 us

profile of v2, /device:TPU:0, one launch (start us, length us, event | category | flops | bytes accessed | tf_op | source)
XLA Modules:
  0.0 51.7 jit_solution(10458640913676567869)
XLA Ops:
  0.6 0.0 copy-start.3
  0.6 0.7 %broadcast_multiply_fusion = s32[512,1]{0,1:T(1,128)S(1)} fusion(s32[512,1]{0,1:T(1,128)} %param.13), kind=kLoop, calls=%fused_computation | loop fusion | flops 512 | bytes 4096 | tf_op jit(solution)/shard_map/mul | solution.py:432
  1.3 0.0 copy-done.3
  1.3 0.6 %add.5 = s32[512]{0:T(512)} add(s32[512]{0:T(512)S(1)} %bitcast.5, s32[512]{0:T(512)S(1)} %copy-done.3) | non-fusion elementwise | flops 512 | bytes 6144 | tf_op jit(solution)/shard_map/add | solution.py:432
  1.9 45.3 %shard_map.137 = (f32[128,512]{1,0:T(8,128)}, f32[128,512]{1,0:T(8,128)}, f32[1,128]{1,0:T(1,128)}, f32[64,1024]{1,0:T(8,128)}, f32[64,256]{1,0:T(8,128)}) custom-call(s32[1,4]{1,0:T(1,128)} %lens.1, bf16[512,512]{1,0:T(8,128)(2,1)} %tokens.1, bf16[512,512]{1,0:T(8,128)(2,1)} %grads.1, s32[1,512]{1,0:T(1,128)} %bitcast.4, bf16[512,1024]{1,0:T(8,128)(2,1)} %w_in.1, ...), custom_call_target="tpu_custom_call" | custom-call | tf_op jit(solution)/shard_map/pallas_call | solution.py:448
  47.2 0.0 copy-start.1
  47.2 1.7 %copy.20 = f32[128,512]{1,0:T(8,128)} copy(f32[128,512]{1,0:T(8,128)} %get-tuple-element.20) | data formatting | bytes 524288
  49.0 0.0 copy-done.1
  49.0 0.0 copy-start.4
  49.0 0.0 copy-start
  49.0 0.7 %copy.21 = f32[128,512]{1,0:T(8,128)} copy(f32[128,512]{1,0:T(8,128)S(1)} %copy-done.1) | data formatting | bytes 524288
  49.7 0.0 copy-done.4
  49.7 0.5 copy.22
  50.2 0.0 copy-done
  50.2 0.0 copy-start.2
  50.2 0.7 %copy.23 = f32[64,1024]{1,0:T(8,128)} copy(f32[64,1024]{1,0:T(8,128)S(1)} %copy-done) | data formatting | bytes 524288
  50.9 0.2 copy-done.2
  51.0 0.6 %copy.24 = f32[64,256]{1,0:T(8,128)} copy(f32[64,256]{1,0:T(8,128)S(1)} %copy-done.2) | data formatting | bytes 131072
Async XLA Ops:
  0.6 0.7 %copy-start.3 = (s32[512]{0:T(512)S(1)}, s32[512]{0:T(512)}, u32[]{:S(2)}) copy-start(s32[512]{0:T(512)} %param.14) | copy-start | bytes 6148
  47.2 1.7 %copy-start.1 = (f32[128,512]{1,0:T(8,128)S(1)}, f32[128,512]{1,0:T(8,128)}, u32[]{:S(2)}) copy-start(f32[128,512]{1,0:T(8,128)} %get-tuple-element.21) | copy-start | bytes 786436
  49.0 0.7 %copy-start.4 = (f32[1,128]{1,0:T(1,128)S(1)}, f32[1,128]{1,0:T(1,128)}, u32[]{:S(2)}) copy-start(f32[1,128]{1,0:T(1,128)} %get-tuple-element.12) | copy-start | bytes 1540
  49.0 1.2 %copy-start = (f32[64,1024]{1,0:T(8,128)S(1)}, f32[64,1024]{1,0:T(8,128)}, u32[]{:S(2)}) copy-start(f32[64,1024]{1,0:T(8,128)} %get-tuple-element.23) | copy-start | bytes 786436
  50.2 0.9 %copy-start.2 = (f32[64,256]{1,0:T(8,128)S(1)}, f32[64,256]{1,0:T(8,128)}, u32[]{:S(2)}) copy-start(f32[64,256]{1,0:T(8,128)} %get-tuple-element.24) | copy-start | bytes 196612
